TPU v7x, 32 devices: a whole 2x2x4 slice. The times are simulated.
32 devices in a mesh: row: 16 (over z, x, core), col: 2 (over y).
Axes of the slice: x: 2, y: 2, z: 4, core: 2. Of those that a mesh axis runs over, the one named last changes fastest.
Arguments:
- gbar: float32 [8192, 8192], P('row', 'col'), may hold values from -9 to 9
- panels: float32 [8192, 1024], P('row'), may hold values from -0.0625 to 0.0625
- panel_cot: float32 [8192, 1024], P('row'), may hold values from -6 to 6
- inverses: float32 [2, 512, 512], replicated, may hold values from -1 to 2, as said below
Outputs:
- adjoint: float32 [8192, 1024], P('row')
- diag_adjoint: float32 [2, 512, 512], P(None, 'row')
Inputs may be any that keep to these rules, and one draw needn't show every extreme that they name: Each inverses[i] is lower triangular with diagonal entries between 1 and 2.
All inputs are finite; a program needn't handle non-finite values.
Results may differ from a plain program's by a relative error of at most 0.000071.
Values sent between devices are 32-bit elements; how exact they have to be, the bound alone decides.
A program may use at most 128 MiB of HBM per device.

v0:
```python
import jax
import jax.numpy as jnp
from jax import lax
from jax.experimental import pallas as pl
from jax.experimental.pallas import tpu as pltpu
from jax.sharding import PartitionSpec as P

MESH = pl.DeviceIdType.MESH
SUBS = 4
PARTS = 2


def halves(value):
    high = value.astype(jnp.bfloat16)
    low = (value - high.astype(jnp.float32)).astype(jnp.bfloat16)
    return high, low


def product(left, right):
    (left_high, left_low), (right_high, right_low) = left, right

    def one(a, b):
        return jnp.dot(a, b, preferred_element_type=jnp.float32)

    return one(left_high, right_low) + one(left_low, right_high) + one(left_high, right_high)


def ring_kernel(
    chips, gbar, panels, cot, inverses,
    adjoint, diag,
    g_v, p_v, cot_t, inv_v, inv_high, inv_low, p_high, p_low, terms, other, arrived, final, adj_v,
    diag_v, diag_mate, diag_parts, diag_out,
    load_sems, out_sems, pair_send, pair_recv, ring_send, ring_recv, end_send, end_recv,
    mate_sems, part_send, part_recv, swap_sems,
):
    width = inverses.shape[-1]
    lane = width // (2 * PARTS)
    piece = lane // SUBS
    total_steps = PARTS * chips
    block = 2 * width // PARTS
    row = lax.axis_index("row")
    col = lax.axis_index("col")
    chip = row // 2
    core = row % 2
    mate = 1 - core
    half = chips // 2

    def place_of(chip_id):
        return jnp.where(chip_id % 2 == 0, chip_id // 2, chips - 1 - chip_id // 2)

    def chip_at(place):
        return jnp.where(place < half, 2 * place, 2 * (chips - 1 - place) + 1)

    place = place_of(chip)
    right = chip_at((place + 1) % chips)
    left = chip_at((place + chips - 1) % chips)

    def tile_at(way, step):
        ahead = jnp.where(way == 0, place + 2 * chips - 1 - step, place + 1 + step)
        return chip_at(ahead % chips)

    def load_g(tile):
        start = pl.multiple_of(tile * width, width)
        return pltpu.make_async_copy(gbar.at[:, pl.ds(start, width)], g_v.at[tile], load_sems.at[tile])

    def load_p(panel):
        columns = slice(panel * width, (panel + 1) * width)
        return pltpu.make_async_copy(
            panels.at[:, columns], p_v.at[:, columns], load_sems.at[chips + panel]
        )

    load_cot = pltpu.make_async_copy(cot, adj_v, load_sems.at[chips + 2])
    load_inv = pltpu.make_async_copy(inverses, inv_v, load_sems.at[chips + 3])
    load_p(0).start()
    for hop in (1, 2, 3):
        load_g(chip_at((place + chips - hop) % chips)).start()
        load_g(chip_at((place + hop) % chips)).start()
    load_g(chip_at((place + half) % chips)).start()
    load_g(chip).start()
    load_p(1).start()
    load_cot.start()
    load_inv.start()

    barrier = pltpu.get_barrier_semaphore()
    friends = [(2 * ((chip + hop) % chips) + core, col) for hop in range(1, chips)] + [
        (2 * chip + mate, col),
        (2 * chip + core, 1 - col),
        (2 * chip + mate, 1 - col),
    ]
    for friend in friends:
        pl.semaphore_signal(barrier, inc=1, device_id=friend, device_id_type=MESH)

    def turn_p(part):
        if part % (PARTS // 2) == 0:
            load_p(part // (PARTS // 2)).wait()
        rows = slice(part * block, (part + 1) * block)
        high, low = halves(p_v[:, rows].T)
        p_high[rows, :] = high
        p_low[rows, :] = low

    def turn_cot(panel):
        if panel == 0:
            load_cot.wait()
        cot_t[panel] = adj_v[:, panel * width:(panel + 1) * width].T

    def turn_inv(panel):
        if panel == 0:
            load_inv.wait()
        high, low = halves(inv_v[panel].T)
        inv_high[panel] = high
        inv_low[panel] = low

    turn_p(0)

    def pair_copy(panel, way, step):
        return pltpu.make_async_remote_copy(
            terms.at[panel, way, step, mate],
            other.at[panel, way, step],
            pair_send.at[panel, way, step],
            pair_recv.at[panel, way, step],
            device_id=(2 * chip + mate, col),
            device_id_type=MESH,
        )

    def ring_copy(panel, way, step, sub):
        target = jnp.where(way == 0, right, left)
        rows = pl.ds(sub * piece, piece)
        return pltpu.make_async_remote_copy(
            terms.at[panel, way, step, core, rows],
            arrived.at[panel, way, step, rows],
            ring_send.at[panel, way, step, sub],
            ring_recv.at[panel, way, step, sub],
            device_id=(2 * target + core, col),
            device_id_type=MESH,
        )

    def end_copy(panel, way, plane, source_core, sub):
        rows = pl.ds(sub * piece, piece)
        return pltpu.make_async_remote_copy(
            terms.at[panel, way, chips - 1, source_core, rows],
            final.at[panel, way, source_core, rows],
            end_send.at[panel, way, plane, sub],
            end_recv.at[panel, way, source_core, sub],
            device_id=(2 * chip + col, col if plane == 0 else 1 - col),
            device_id_type=MESH,
        )

    def end_local(panel, way, source_core, sub):
        rows = pl.ds(sub * piece, piece)
        return pltpu.make_async_copy(
            terms.at[panel, way, chips - 1, source_core, rows],
            final.at[panel, way, source_core, rows],
            end_recv.at[panel, way, source_core, sub],
        )

    def make_terms(count):
        panel, step = count // chips, count % chips
        for way in (0, 1):
            tile = tile_at(way, step)

            @pl.when((panel == 0) & (step < half if way == 0 else step < half - 1))
            def _():
                load_g(tile).wait()

            @pl.when((panel == 0) & (step == chips - 1) & (way == 0))
            def _():
                load_g(tile).wait()

            rows = pl.ds(pl.multiple_of(panel * block + way * (block // 2), block // 2), block // 2)
            value = product((p_high[rows, :], p_low[rows, :]), halves(g_v[tile]))
            terms[panel, way, step, 0] = value[:lane]
            terms[panel, way, step, 1] = value[lane:]
            pair_copy(panel, way, step).start()

    def ring_step(count):
        panel, step = count // chips, count % chips
        for way in (0, 1):
            pair_copy(panel, way, step).wait_recv()
        for sub in range(SUBS):
            rows = pl.ds(sub * piece, piece)
            for way in (0, 1):
                @pl.when(step > 0)
                def _():
                    ring_copy(panel, way, step - 1, sub).wait_recv()
                    terms[panel, way, step, core, rows] = (
                        terms[panel, way, step, core, rows]
                        + other[panel, way, step, rows]
                        + arrived[panel, way, step - 1, rows]
                    )

                @pl.when(step == 0)
                def _():
                    terms[panel, way, step, core, rows] = (
                        terms[panel, way, step, core, rows] + other[panel, way, step, rows]
                    )

                @pl.when(step < chips - 1)
                def _():
                    ring_copy(panel, way, step, sub).start()

                @pl.when(step == chips - 1)
                def _():
                    end_copy(panel, way, 1, core, sub).start()

                @pl.when((step == chips - 1) & (core == col))
                def _():
                    end_local(panel, way, core, sub).start()

                @pl.when((step == chips - 1) & (core != col))
                def _():
                    end_copy(panel, way, 0, core, sub).start()

    side = pl.ds(pl.multiple_of(col * (width // 2), width // 2), width // 2)
    short = width // (2 * chips)

    def mate_copy(panel):
        return pltpu.make_async_remote_copy(
            diag_v.at[panel, :, mate],
            diag_mate.at[panel],
            mate_sems.at[0, panel],
            mate_sems.at[1, panel],
            device_id=(2 * chip + mate, col),
            device_id_type=MESH,
        )

    def part_copy(panel, source, target):
        return pltpu.make_async_remote_copy(
            diag_v.at[panel, target, core],
            diag_parts.at[panel, source],
            part_send.at[panel, target],
            part_recv.at[panel, source],
            device_id=(2 * target + core, col),
            device_id_type=MESH,
        )

    def swap_copy(panel):
        return pltpu.make_async_remote_copy(
            diag_out.at[panel, :, side],
            diag_out.at[panel, :, side],
            swap_sems.at[0, panel],
            swap_sems.at[1, panel],
            device_id=(2 * chip + core, 1 - col),
            device_id_type=MESH,
        )

    def adjoint_out(panel):
        columns = slice(panel * width, (panel + 1) * width)
        return pltpu.make_async_copy(adj_v.at[:, columns], adjoint.at[:, columns], out_sems.at[panel])

    def solve(panel):
        for part in range(panel * PARTS // 2, (panel + 1) * PARTS // 2):
            for way in (0, 1):
                for source in (0, 1):
                    for sub in range(SUBS):
                        end_local(part, way, source, sub).wait()
        coupled = final[panel * PARTS // 2:(panel + 1) * PARTS // 2].reshape(width, width)
        turned = product((inv_high[panel], inv_low[panel]), halves(cot_t[panel] - 2.0 * coupled))
        cot_t[panel] = turned

    def diagonal(panel):
        start = pl.multiple_of(panel * width + col * (width // 2), width // 2)
        own = p_v[:, pl.ds(start, width // 2)]
        value = -product(halves(cot_t[panel]), halves(own))
        diag_v[panel] = value.reshape(chips, 2, short, width // 2)
        mate_copy(panel).start()

    def give(panel):
        adj_v[:, panel * width:(panel + 1) * width] = cot_t[panel].T
        adjoint_out(panel).start()

    def scatter(panel):
        mate_copy(panel).wait_recv()
        diag_v[panel, :, core] = diag_v[panel, :, core] + diag_mate[panel]
        for hop in range(1, chips):
            part_copy(panel, chip, (chip + hop) % chips).start()

    def collect(panel):
        total = diag_v[panel, chip, core]
        for hop in range(1, chips):
            source = (chip + hop) % chips
            part_copy(panel, source, chip).wait_recv()
            total = total + diag_parts[panel, source]
        diag_out[panel, :, side] = total
        swap_copy(panel).start()

    pl.semaphore_wait(barrier, len(friends))
    make_terms(jnp.int32(0))
    ring_step(jnp.int32(0))
    make_terms(jnp.int32(1))
    make_terms(jnp.int32(2))
    second = total_steps // 2
    chores = {
        1: lambda: turn_p(1),
        2: lambda: turn_cot(0),
        3: lambda: turn_cot(1),
        4: lambda: turn_inv(0),
        5: lambda: turn_inv(1),
        second + 2: lambda: solve(0),
        second + 3: lambda: diagonal(0),
        second + 5: lambda: give(0),
        second + 4: lambda: scatter(0),
        second + 6: lambda: collect(0),
    }

    def body(count, carry):
        @pl.when(count < total_steps - 2)
        def _():
            make_terms(count + 2)

        step = count % chips
        early = (step == chips - 1) & (count < total_steps - 1)
        ring_step(jnp.where(early, count + 1, jnp.where(step == 0, count - 1, count)))
        for at, chore in chores.items():
            pl.when(count == at)(chore)
        return carry

    lax.fori_loop(1, total_steps, body, 0)
    solve(1)
    diagonal(1)
    scatter(1)
    give(1)
    collect(1)

    def drain(count, carry):
        panel, step = count // chips, count % chips
        for way in (0, 1):
            pair_copy(panel, way, step).wait_send()

            @pl.when(step < chips - 1)
            def _():
                for sub in range(SUBS):
                    ring_copy(panel, way, step, sub).wait_send()

        return carry

    lax.fori_loop(0, total_steps, drain, 0)
    for part in range(PARTS):
        for way in (0, 1):
            for sub in range(SUBS):
                end_copy(part, way, 1, core, sub).wait_send()

                @pl.when(core != col)
                def _():
                    end_copy(part, way, 0, core, sub).wait_send()

    for panel in (0, 1):
        mate_copy(panel).wait_send()
        for hop in range(1, chips):
            part_copy(panel, chip, (chip + hop) % chips).wait_send()
        swap_copy(panel).wait()
        adjoint_out(panel).wait()
    store = pltpu.make_async_copy(diag_out, diag, out_sems.at[2])
    store.start()
    store.wait()


def ring_device(gbar, panels, panel_cot, inverses):
    width = inverses.shape[-1]
    chips = lax.axis_size("row") // 2
    lane = width // (2 * PARTS)
    f32, dma = jnp.float32, pltpu.SemaphoreType.DMA
    anywhere = pl.BlockSpec(memory_space=pl.ANY)

    def kernel(*refs):
        ring_kernel(chips, *refs)

    short = width // (2 * chips)
    bf16 = jnp.bfloat16
    return pl.pallas_call(
        kernel,
        out_shape=(
            jax.ShapeDtypeStruct(panels.shape, f32),
            jax.ShapeDtypeStruct((2, short, width), f32),
        ),
        in_specs=[anywhere] * 4,
        out_specs=(anywhere, anywhere),
        scratch_shapes=[
            pltpu.VMEM((chips, width, width), f32),
            pltpu.VMEM(panels.shape, f32),
            pltpu.VMEM(inverses.shape, f32),
            pltpu.VMEM(inverses.shape, f32),
            pltpu.VMEM(inverses.shape, bf16),
            pltpu.VMEM(inverses.shape, bf16),
            pltpu.VMEM((2 * width, width), bf16),
            pltpu.VMEM((2 * width, width), bf16),
            pltpu.VMEM((PARTS, 2, chips, 2, lane, width), f32),
            pltpu.VMEM((PARTS, 2, chips, lane, width), f32),
            pltpu.VMEM((PARTS, 2, chips - 1, lane, width), f32),
            pltpu.VMEM((PARTS, 2, 2, lane, width), f32),
            pltpu.VMEM(panels.shape, f32),
            pltpu.VMEM((2, chips, 2, short, width // 2), f32),
            pltpu.VMEM((2, chips, short, width // 2), f32),
            pltpu.VMEM((2, chips, short, width // 2), f32),
            pltpu.VMEM((2, short, width), f32),
            dma((chips + 4,)),
            dma((3,)),
            dma((PARTS, 2, chips)),
            dma((PARTS, 2, chips)),
            dma((PARTS, 2, chips - 1, SUBS)),
            dma((PARTS, 2, chips - 1, SUBS)),
            dma((PARTS, 2, 2, SUBS)),
            dma((PARTS, 2, 2, SUBS)),
            dma((2, 2)),
            dma((2, chips)),
            dma((2, chips)),
            dma((2, 2)),
        ],
        compiler_params=pltpu.CompilerParams(
            collective_id=0, has_side_effects=True, vmem_limit_bytes=62 * 1024 * 1024
        ),
    )(gbar, panels, panel_cot, inverses)


def plain_device(gbar, panels, panel_cot, inverses):
    width = inverses.shape[-1]
    mode = lax.Precision.HIGHEST
    row_id = lax.axis_index("row")
    col_count = lax.axis_size("col")
    contract = (((0,), (0,)), ((), ()))
    partial_value = lax.dot_general(
        gbar, panels, contract, precision=mode, preferred_element_type=jnp.float32
    )
    summed = lax.psum(partial_value, "row")
    own_tile = lax.dynamic_slice_in_dim(summed, row_id // col_count * width, width, 0)
    own_tile = jnp.where(lax.axis_index("col") == row_id % col_count, own_tile, 0)
    combined = panel_cot - 2.0 * lax.psum(own_tile, "col")
    adjoint, terms = [], []
    for panel in (0, 1):
        columns = slice(panel * width, (panel + 1) * width)
        adjoint.append(
            jnp.dot(combined[:, columns], inverses[panel], precision=mode, preferred_element_type=jnp.float32)
        )
        terms.append(
            -lax.dot_general(
                adjoint[-1], panels[:, columns], contract, precision=mode, preferred_element_type=jnp.float32
            )
        )
    diag_adjoint = lax.psum_scatter(jnp.stack(terms), "row", scatter_dimension=1, tiled=True)
    return jnp.concatenate(adjoint, axis=1), diag_adjoint


def solution(mesh):
    in_specs = (P("row", "col"), P("row", None), P("row", None), P())
    out_specs = (P("row", None), P(None, "row", None))
    on_ring = mesh.shape["col"] == 2 and mesh.shape["row"] == 16
    return jax.shard_map(
        ring_device if on_ring else plain_device,
        mesh=mesh, in_specs=in_specs, out_specs=out_specs, check_vma=False,
    )
```

profile of v0, /device:TPU:0, one launch (start us, length us, event | category | flops | bytes accessed | tf_op | source)
XLA Modules:
  0.0 121.6 jit_solution(3947584780854882728)
XLA Ops:
  0.6 117.1 %shard_map.59 = (f32[512,1024]{1,0:T(8,128)}, f32[2,32,512]{2,1,0:T(8,128)}) custom-call(f32[512,4096]{1,0:T(8,128)} %refs_0_.1, f32[512,1024]{1,0:T(8,128)} %refs_1_.1, f32[512,1024]{1,0:T(8,128)} %refs_2_.1, f32[2,512,512]{2,1,0:T(8,128)} %refs_3_.1), custom_call_target="tpu_custom_call" | custom-call | tf_op jit(solution)/shard_map/pallas_call | solution.py:369
  117.7 0.0 copy-start
  117.8 3.2 %copy.8 = f32[512,1024]{1,0:T(8,128)} copy(f32[512,1024]{1,0:T(8,128)} %get-tuple-element.4) | data formatting | bytes 4194304
  120.9 0.0 copy-done
  120.9 0.7 copy.9
Async XLA Ops:
  117.7 3.2 %copy-start = (f32[2,32,512]{2,1,0:T(8,128)S(1)}, f32[2,32,512]{2,1,0:T(8,128)}, u32[]{:S(2)}) copy-start(f32[2,32,512]{2,1,0:T(8,128)} %get-tuple-element.5) | copy-start | bytes 393220
where the time goes:
time: 122 us
  Pallas kernels  117 us (96%)
  local copies, waits for them, and re-layouts  3.85 us (3%)
    pallas_call x1, Pallas kernels, ring_device(): pl.pallas_call(kernel, out_shape=(jax.ShapeDtypeStruct(panels.shape, f32)...  117 us
    unnamed x4, local copies, waits for them, and re-layouts  3.85 us

commit v1 on v0

v1 whole, which is shorter than its diff:
```python
import jax
import jax.numpy as jnp
from jax import lax
from jax.experimental import pallas as pl
from jax.experimental.pallas import tpu as pltpu
from jax.sharding import PartitionSpec as P

MESH = pl.DeviceIdType.MESH
SUBS = 4
UP, DOWN, ACROSS = 0, 1, 2


def halves(value):
    high = value.astype(jnp.bfloat16)
    low = (value - high.astype(jnp.float32)).astype(jnp.bfloat16)
    return high, low


def product(left, right):
    (left_high, left_low), (right_high, right_low) = left, right

    def one(a, b):
        return jnp.dot(a, b, preferred_element_type=jnp.float32)

    return one(left_high, right_low) + one(left_low, right_high) + one(left_high, right_high)


def ladder_kernel(
    nz, gbar, panels, cot, inverses,
    adjoint, diag,
    g_v, p_v, gath, terms, other, zin_pair, zin_one, xin_one, xin_last, final,
    acc, acc_other, p_high, p_low, inv_v, cot_t, adj_v,
    diag_v, diag_mate, diag_parts, diag_out,
    load_sems, own_sems, out_sems,
    gath_send, gath_far, gath_recv, gath_mate,
    term_sems, xone_sems, pair_send, pair_recv, one_send, one_recv, last_sems,
    end_send, end_recv, acc_sems,
    mate_sems, part_send, part_recv, swap_sems,
):
    width = inverses.shape[-1]
    chips = 2 * nz
    half = width // 2
    lane = width // 4
    piece = lane // SUBS
    row = lax.axis_index("row")
    col = lax.axis_index("col")
    chip = row // 2
    core = row % 2
    mate = 1 - core
    x = chip % 2
    z = chip // 2
    across = 2 * z + 1 - x

    def port_chip(port):
        if port == ACROSS:
            return across
        return chip + 2 - 4 * port

    def has_next(port):
        return jnp.where(port == UP, z < nz - 1, z > 0)

    def has_prev(port):
        return jnp.where(port == UP, z > 0, z < nz - 1)

    def behind(port, step):
        return z - step + 2 * step * port

    def ahead(port, step):
        return z + step - 2 * step * port

    def inside(place):
        return (place >= 0) & (place < nz)

    def load_g(tile):
        start = pl.multiple_of(tile * width, width)
        return pltpu.make_async_copy(gbar.at[:, pl.ds(start, width)], g_v.at[tile], load_sems.at[tile])

    def load_p(panel):
        columns = slice(panel * width, (panel + 1) * width)
        return pltpu.make_async_copy(panels.at[:, columns], p_v.at[:, columns], load_sems.at[chips + panel])

    def load_own(side):
        columns = slice(side * half, (side + 1) * half)
        return pltpu.make_async_copy(panels.at[:, columns], gath.at[chip, side], own_sems.at[side])

    load_cot = pltpu.make_async_copy(cot, adj_v, load_sems.at[chips + 2])
    load_inv = pltpu.make_async_copy(inverses, inv_v, load_sems.at[chips + 3])

    def order(count):
        place = jnp.where(z < nz // 2, nz - 1 - count // 2, count // 2)
        return 2 * place + jnp.where(count % 2 == 0, 1 - x, x)

    @pl.when(core == col)
    def _():
        load_own(1).start()
        load_own(0).start()

    load_p(1).start()
    for count in range(chips):
        load_g(order(count)).start()
    load_p(0).start()
    load_cot.start()
    load_inv.start()

    barrier = pltpu.get_barrier_semaphore()
    friends = [(2 * ((chip + hop) % chips) + lead, col) for hop in range(1, chips) for lead in (0, 1)] + [
        (2 * chip + mate, col),
        (2 * chip + core, 1 - col),
        (2 * chip + mate, 1 - col),
    ]
    for friend in friends:
        pl.semaphore_signal(barrier, inc=1, device_id=friend, device_id_type=MESH)

    load_p(1).wait()
    for part in (0, 1):
        rows = slice(part * half, (part + 1) * half)
        high, low = halves(p_v[:, width + part * half:width + (part + 1) * half].T)
        p_high[rows, :] = high
        p_low[rows, :] = low
    pl.semaphore_wait(barrier, len(friends))

    def gather_copy(tile, side, port, lead, far):
        rows = pl.ds(pl.multiple_of(lead * half, half), half)
        return pltpu.make_async_remote_copy(
            gath.at[tile, side, rows],
            gath.at[tile, side, rows],
            gath_far.at[port, side] if far else gath_send.at[port, tile, side],
            gath_recv.at[tile, side],
            device_id=(2 * port_chip(port) + lead, col),
            device_id_type=MESH,
        )

    def gather_pair(tile, side):
        rows = pl.ds(pl.multiple_of(core * half, half), half)
        return pltpu.make_async_remote_copy(
            gath.at[tile, side, rows],
            gath.at[tile, side, rows],
            gath_mate.at[0, tile, side],
            gath_mate.at[1, tile, side],
            device_id=(2 * chip + mate, col),
            device_id_type=MESH,
        )

    def gather_own_pair(side):
        return pltpu.make_async_remote_copy(
            gath.at[chip, side],
            gath.at[chip, side],
            gath_mate.at[0, chip, side],
            gath_mate.at[1, chip, side],
            device_id=(2 * chip + mate, col),
            device_id_type=MESH,
        )

    def own_sends(act):
        def one(side, port):
            def go():
                act(gather_copy(chip, side, port, core, False))
                act(gather_copy(chip, side, port, mate, True))

            if port == ACROSS:
                go()
            else:
                pl.when(has_next(port))(go)

        @pl.when(core == col)
        def _():
            one(0, ACROSS)
            for side in (1, 0):
                for port in (UP, DOWN):
                    one(side, port)
            one(1, ACROSS)
            act(gather_own_pair(0))
            act(gather_own_pair(1))

    def relay(tile, side, ports, act):
        for port in ports:
            if port == ACROSS:
                act(gather_copy(tile, side, port, core, False))
            else:
                @pl.when(has_next(port))
                def _():
                    act(gather_copy(tile, side, port, core, False))
        act(gather_pair(tile, side))

    def arrived(tile, side):
        gather_copy(tile, side, ACROSS, core, False).wait_recv()

    def start(copy):
        copy.start()

    def finish(copy):
        copy.wait_send()

    def relay_b(step, act):
        for port in (UP, DOWN):
            place = behind(port, step)

            @pl.when(inside(place))
            def _():
                tile = 2 * place + x
                if act is start:
                    arrived(tile, 1)
                relay(tile, 1, (port, ACROSS), act)

    def relay_a(step, act, own):
        for port in (UP, DOWN):
            place = behind(port, step)

            @pl.when(inside(place))
            def _():
                tile = 2 * place + (x if own else 1 - x)
                if act is start:
                    arrived(tile, 0)
                relay(tile, 0, (port,), act)

    def relay_a_across(act):
        if act is start:
            arrived(across, 0)
        relay(across, 0, (UP, DOWN), act)

    def relay_bx(step, act):
        for port in (UP, DOWN) if step else (UP,):
            place = behind(port, step)

            @pl.when(inside(place))
            def _():
                tile = 2 * place + 1 - x
                if act is start:
                    arrived(tile, 1)
                relay(tile, 1, (), act)

    def forward(tile, side):
        @pl.when((tile != chip) | (core != col))
        def _():
            gather_pair_wait(tile, side)

        acc[side] += product(halves(g_v[tile]), halves(gath[tile, side]))

    def gather_pair_wait(tile, side):
        @pl.when(tile == chip)
        def _():
            gather_own_pair(side).wait_recv()

        @pl.when(tile != chip)
        def _():
            gather_pair(tile, side).wait_recv()

    def forward_step(step, kinds):
        def both(port, carry):
            place = behind(port, step)

            @pl.when(inside(place))
            def _():
                for side, own in kinds:
                    forward(2 * place + (x if own else 1 - x), side)

            return carry

        lax.fori_loop(0, 2 if step else 1, both, 0)

    def term_copy(tile):
        return pltpu.make_async_remote_copy(
            terms.at[tile, :, mate],
            other.at[tile],
            term_sems.at[0, tile],
            term_sems.at[1, tile],
            device_id=(2 * chip + mate, col),
            device_id_type=MESH,
        )

    def xone_copy(place, tile):
        return pltpu.make_async_remote_copy(
            terms.at[tile, 1, core],
            xin_one.at[place],
            xone_sems.at[0, place],
            xone_sems.at[1, place],
            device_id=(2 * across + core, col),
            device_id_type=MESH,
        )

    def make_terms(count):
        tile = order(count)
        load_g(tile).wait()
        for part in (0, 1):
            rows = slice(part * half, (part + 1) * half)
            value = product((p_high[rows, :], p_low[rows, :]), halves(g_v[tile]))
            terms[tile, part] = value.reshape(2, lane, width)
        term_copy(tile).start()

    def pair_terms(count):
        tile = order(count)
        term_copy(tile).wait_recv()
        terms[tile, :, core] = terms[tile, :, core] + other[tile]

        @pl.when(count == 0)
        def _():
            xone_copy(tile // 2, tile).start()

    def send_across(count):
        tile = order(count)
        xone_copy(tile // 2, tile).start()

    def pair_copy(port, step, slot, tile, sub):
        rows = pl.ds(sub * piece, piece)
        return pltpu.make_async_remote_copy(
            terms.at[tile, 0, core, rows],
            zin_pair.at[port, step - 1, slot, rows],
            pair_send.at[port, step - 1, slot, sub],
            pair_recv.at[port, step - 1, slot, sub],
            device_id=(2 * port_chip(port) + core, col),
            device_id_type=MESH,
        )

    def one_copy(port, step, tile, sub):
        rows = pl.ds(sub * piece, piece)
        return pltpu.make_async_remote_copy(
            terms.at[tile, 1, core, rows],
            zin_one.at[port, step - 1, rows],
            one_send.at[port, step - 1, sub],
            one_recv.at[port, step - 1, sub],
            device_id=(2 * port_chip(port) + core, col),
            device_id_type=MESH,
        )

    def sum_pair(step):
        for slot in (0, 1):
            for port in (UP, DOWN):
                place = ahead(port, step)

                @pl.when(inside(place))
                def _():
                    tile = 2 * place + (x if slot else 1 - x)

                    def each(sub, carry):
                        rows = pl.ds(pl.multiple_of(sub * piece, piece), piece)
                        if step < nz - 1:
                            @pl.when(has_prev(port))
                            def _():
                                pair_copy(port, step + 1, slot, tile, sub).wait_recv()
                                terms[tile, 0, core, rows] = (
                                    terms[tile, 0, core, rows] + zin_pair[port, step, slot, rows]
                                )

                        pair_copy(port, step, slot, tile, sub).start()
                        return carry

                    lax.fori_loop(0, SUBS, each, 0)

    def sum_one(step):
        for port in (UP, DOWN):
            place = ahead(port, step)

            @pl.when(inside(place))
            def _():
                tile = 2 * place + x
                xone_copy(place, tile).wait_recv()

                def each(sub, carry):
                    rows = pl.ds(pl.multiple_of(sub * piece, piece), piece)
                    value = terms[tile, 1, core, rows] + xin_one[place, rows]
                    terms[tile, 1, core, rows] = value
                    if step < nz - 1:
                        @pl.when(has_prev(port))
                        def _():
                            one_copy(port, step + 1, tile, sub).wait_recv()
                            terms[tile, 1, core, rows] = value + zin_one[port, step, rows]

                    one_copy(port, step, tile, sub).start()
                    return carry

                lax.fori_loop(0, SUBS, each, 0)

    def last_copy(sub):
        rows = pl.ds(sub * piece, piece)
        return pltpu.make_async_remote_copy(
            terms.at[across, 0, core, rows],
            xin_last.at[rows],
            last_sems.at[0, sub],
            last_sems.at[1, sub],
            device_id=(2 * across + core, col),
            device_id_type=MESH,
        )

    def end_copy(part, plane, source_core, sub):
        rows = pl.ds(sub * piece, piece)
        return pltpu.make_async_remote_copy(
            terms.at[chip, part, source_core, rows],
            final.at[part, source_core, rows],
            end_send.at[part, plane, sub],
            end_recv.at[part, source_core, sub],
            device_id=(2 * chip + col, col if plane == 0 else 1 - col),
            device_id_type=MESH,
        )

    def end_local(part, source_core, sub):
        rows = pl.ds(sub * piece, piece)
        return pltpu.make_async_copy(
            terms.at[chip, part, source_core, rows],
            final.at[part, source_core, rows],
            end_recv.at[part, source_core, sub],
        )

    def give_end(part, sub):
        end_copy(part, 1, core, sub).start()

        @pl.when(core == col)
        def _():
            end_local(part, core, sub).start()

        @pl.when(core != col)
        def _():
            end_copy(part, 0, core, sub).start()

    def last_pair(sub, carry):
        rows = pl.ds(pl.multiple_of(sub * piece, piece), piece)
        for slot in (0, 1):
            tile = chip if slot else across
            for port in (UP, DOWN):
                @pl.when(has_prev(port))
                def _():
                    pair_copy(port, 1, slot, tile, sub).wait_recv()
                    terms[tile, 0, core, rows] = terms[tile, 0, core, rows] + zin_pair[port, 0, slot, rows]

            if slot == 0:
                last_copy(sub).start()
        return carry

    def last_across(sub, carry):
        rows = pl.ds(pl.multiple_of(sub * piece, piece), piece)
        last_copy(sub).wait_recv()
        terms[chip, 0, core, rows] = terms[chip, 0, core, rows] + xin_last[rows]
        give_end(0, sub)
        return carry

    def last_one(sub, carry):
        rows = pl.ds(pl.multiple_of(sub * piece, piece), piece)
        terms[chip, 1, core, rows] = terms[chip, 1, core, rows] + xin_one[z, rows]
        for port in (UP, DOWN):
            @pl.when(has_prev(port))
            def _():
                one_copy(port, 1, chip, sub).wait_recv()
                terms[chip, 1, core, rows] = terms[chip, 1, core, rows] + zin_one[port, 0, rows]

        give_end(1, sub)
        return carry

    def acc_copy(side):
        return pltpu.make_async_remote_copy(
            acc.at[side],
            acc_other.at[side],
            acc_sems.at[0, side],
            acc_sems.at[1, side],
            device_id=(2 * chip + core, 1 - col),
            device_id_type=MESH,
        )

    side_columns = pl.ds(pl.multiple_of(col * half, half), half)
    short = width // (2 * chips)

    def mate_copy(panel):
        return pltpu.make_async_remote_copy(
            diag_v.at[panel, :, mate],
            diag_mate.at[panel],
            mate_sems.at[0, panel],
            mate_sems.at[1, panel],
            device_id=(2 * chip + mate, col),
            device_id_type=MESH,
        )

    def part_copy(panel, source, target):
        return pltpu.make_async_remote_copy(
            diag_v.at[panel, target, core],
            diag_parts.at[panel, source],
            part_send.at[panel, target],
            part_recv.at[panel, source],
            device_id=(2 * target + core, col),
            device_id_type=MESH,
        )

    def swap_copy(panel):
        return pltpu.make_async_remote_copy(
            diag_out.at[panel, :, side_columns],
            diag_out.at[panel, :, side_columns],
            swap_sems.at[0, panel],
            swap_sems.at[1, panel],
            device_id=(2 * chip + core, 1 - col),
            device_id_type=MESH,
        )

    def adjoint_out(panel):
        columns = slice(panel * width, (panel + 1) * width)
        return pltpu.make_async_copy(adj_v.at[:, columns], adjoint.at[:, columns], out_sems.at[panel])

    def solve_first():
        for side in (0, 1):
            acc_copy(side).wait_recv()
        for side in (0, 1):
            columns = slice(side * half, (side + 1) * half)
            cot_t[0, :, columns] = adj_v[:, columns] - 2.0 * (acc[side] + acc_other[side])
        turned = product(halves(cot_t[0]), halves(inv_v[0]))
        adj_v[:, :width] = turned
        adjoint_out(0).start()
        cot_t[0] = turned.T

    def solve_second():
        for part in (0, 1):
            for source in (0, 1):
                for sub in range(SUBS):
                    end_local(part, source, sub).wait()
        coupled = final[...].reshape(width, width)
        cot_t[1] = product(halves(inv_v[1]), halves(cot_t[1] - 2.0 * coupled))

    def diagonal(panel):
        place = pl.multiple_of(panel * width + col * half, half)
        own = p_v[:, pl.ds(place, half)]
        value = -product(halves(cot_t[panel]), halves(own))
        diag_v[panel] = value.reshape(chips, 2, short, half)
        mate_copy(panel).start()

    def give_second():
        adj_v[:, width:] = cot_t[1].T
        adjoint_out(1).start()

    def scatter(panel):
        mate_copy(panel).wait_recv()
        diag_v[panel, :, core] = diag_v[panel, :, core] + diag_mate[panel]
        for hop in range(1, chips):
            part_copy(panel, chip, (chip + hop) % chips).start()

    def collect(panel):
        total = diag_v[panel, chip, core]
        for hop in range(1, chips):
            source = (chip + hop) % chips
            part_copy(panel, source, chip).wait_recv()
            total = total + diag_parts[panel, source]
        diag_out[panel, :, side_columns] = total
        swap_copy(panel).start()

    def turn_cot():
        cot_t[1] = adj_v[:, width:].T

    def turn_inv():
        inv_v[1] = inv_v[1].T

    @pl.when(core == col)
    def _():
        load_own(1).wait()
        load_own(0).wait()

    own_sends(start)
    acc[...] = jnp.zeros_like(acc)
    chores = {
        4: lambda: relay_a_across(start),
        7: lambda: relay_b(1, start),
    }

    def produce(count, carry):
        make_terms(count)
        pl.when(count > 0)(lambda: pair_terms(count - 1))
        for at, chore in chores.items():
            pl.when(count == at)(chore)
        return carry

    lax.fori_loop(0, chips, produce, 0)
    pair_terms(jnp.int32(chips - 1))

    relay_a(1, start, True)
    sum_pair(3)
    forward_step(0, [(0, True), (1, True)])
    forward_step(1, [(0, True), (1, True)])
    relay_b(2, start)
    sum_one(3)
    relay_a(1, start, False)
    forward_step(1, [(0, False)])
    forward_step(0, [(0, False)])
    send_across(2)
    sum_pair(2)
    relay_b(3, start)
    forward_step(2, [(1, True)])
    relay_a(2, start, True)
    send_across(4)
    forward_step(2, [(0, True)])
    forward_step(3, [(1, True)])
    relay_bx(0, start)
    relay_bx(1, start)
    forward_step(0, [(1, False)])
    forward_step(1, [(1, False)])
    relay_a(2, start, False)
    sum_one(2)
    relay_bx(2, start)
    relay_bx(3, start)
    forward_step(2, [(1, False)])
    forward_step(3, [(1, False)])
    acc_copy(1).start()
    send_across(6)
    forward_step(2, [(0, False)])
    sum_pair(1)
    load_p(0).wait()
    load_cot.wait()
    load_inv.wait()
    turn_cot()
    turn_inv()
    relay_a(3, start, True)
    relay_a(3, start, False)
    forward_step(3, [(0, True), (0, False)])
    acc_copy(0).start()
    sum_one(1)
    lax.fori_loop(0, SUBS, last_pair, 0)
    lax.fori_loop(0, SUBS, last_across, 0)
    xone_copy(z, chip).wait_recv()
    lax.fori_loop(0, SUBS, last_one, 0)
    solve_first()
    diagonal(0)
    scatter(0)
    solve_second()
    diagonal(1)
    collect(0)
    scatter(1)
    give_second()
    collect(1)

    own_sends(finish)
    relay_a_across(finish)
    relay_bx(0, finish)

    def drain_terms(count, carry):
        tile = order(count)
        term_copy(tile).wait_send()

        @pl.when(tile % 2 != x)
        def _():
            xone_copy(tile // 2, tile).wait_send()

        return carry

    lax.fori_loop(0, chips, drain_terms, 0)
    for step in range(1, nz):
        relay_b(step, finish)
        relay_a(step, finish, True)
        relay_a(step, finish, False)
        relay_bx(step, finish)
        for port in (UP, DOWN):
            place = ahead(port, step)

            @pl.when(inside(place))
            def _():
                for sub in range(SUBS):
                    for slot in (0, 1):
                        pair_copy(port, step, slot, 2 * place + (x if slot else 1 - x), sub).wait_send()
                    one_copy(port, step, 2 * place + x, sub).wait_send()

    for sub in range(SUBS):
        last_copy(sub).wait_send()
        for part in (0, 1):
            end_copy(part, 1, core, sub).wait_send()

            @pl.when(core != col)
            def _():
                end_copy(part, 0, core, sub).wait_send()

    for panel in (0, 1):
        acc_copy(panel).wait_send()
        mate_copy(panel).wait_send()
        for hop in range(1, chips):
            part_copy(panel, chip, (chip + hop) % chips).wait_send()
        swap_copy(panel).wait()
        adjoint_out(panel).wait()
    store = pltpu.make_async_copy(diag_out, diag, out_sems.at[2])
    store.start()
    store.wait()


def ladder_device(gbar, panels, panel_cot, inverses):
    width = inverses.shape[-1]
    chips = lax.axis_size("row") // 2
    nz = chips // 2
    half, lane = width // 2, width // 4
    short = width // (2 * chips)
    f32, bf16, dma = jnp.float32, jnp.bfloat16, pltpu.SemaphoreType.DMA
    anywhere = pl.BlockSpec(memory_space=pl.ANY)

    def kernel(*refs):
        ladder_kernel(nz, *refs)

    return pl.pallas_call(
        kernel,
        out_shape=(
            jax.ShapeDtypeStruct(panels.shape, f32),
            jax.ShapeDtypeStruct((2, short, width), f32),
        ),
        in_specs=[anywhere] * 4,
        out_specs=(anywhere, anywhere),
        scratch_shapes=[
            pltpu.VMEM((chips, width, width), f32),
            pltpu.VMEM(panels.shape, f32),
            pltpu.VMEM((chips, 2, width, half), f32),
            pltpu.VMEM((chips, 2, 2, lane, width), f32),
            pltpu.VMEM((chips, 2, lane, width), f32),
            pltpu.VMEM((2, nz - 1, 2, lane, width), f32),
            pltpu.VMEM((2, nz - 1, lane, width), f32),
            pltpu.VMEM((nz, lane, width), f32),
            pltpu.VMEM((lane, width), f32),
            pltpu.VMEM((2, 2, lane, width), f32),
            pltpu.VMEM((2, width, half), f32),
            pltpu.VMEM((2, width, half), f32),
            pltpu.VMEM((width, width), bf16),
            pltpu.VMEM((width, width), bf16),
            pltpu.VMEM(inverses.shape, f32),
            pltpu.VMEM(inverses.shape, f32),
            pltpu.VMEM(panels.shape, f32),
            pltpu.VMEM((2, chips, 2, short, half), f32),
            pltpu.VMEM((2, chips, short, half), f32),
            pltpu.VMEM((2, chips, short, half), f32),
            pltpu.VMEM((2, short, width), f32),
            dma((chips + 4,)),
            dma((2,)),
            dma((3,)),
            dma((3, chips, 2)),
            dma((3, 2)),
            dma((chips, 2)),
            dma((2, chips, 2)),
            dma((2, chips)),
            dma((2, nz)),
            dma((2, nz - 1, 2, SUBS)),
            dma((2, nz - 1, 2, SUBS)),
            dma((2, nz - 1, SUBS)),
            dma((2, nz - 1, SUBS)),
            dma((2, SUBS)),
            dma((2, 2, SUBS)),
            dma((2, 2, SUBS)),
            dma((2, 2)),
            dma((2, 2)),
            dma((2, chips)),
            dma((2, chips)),
            dma((2, 2)),
        ],
        compiler_params=pltpu.CompilerParams(
            collective_id=0, has_side_effects=True, vmem_limit_bytes=62 * 1024 * 1024
        ),
    )(gbar, panels, panel_cot, inverses)


def plain_device(gbar, panels, panel_cot, inverses):
    width = inverses.shape[-1]
    mode = lax.Precision.HIGHEST
    row_id = lax.axis_index("row")
    col_count = lax.axis_size("col")
    contract = (((0,), (0,)), ((), ()))
    partial_value = lax.dot_general(
        gbar, panels, contract, precision=mode, preferred_element_type=jnp.float32
    )
    summed = lax.psum(partial_value, "row")
    own_tile = lax.dynamic_slice_in_dim(summed, row_id // col_count * width, width, 0)
    own_tile = jnp.where(lax.axis_index("col") == row_id % col_count, own_tile, 0)
    combined = panel_cot - 2.0 * lax.psum(own_tile, "col")
    adjoint, terms = [], []
    for panel in (0, 1):
        columns = slice(panel * width, (panel + 1) * width)
        adjoint.append(
            jnp.dot(combined[:, columns], inverses[panel], precision=mode, preferred_element_type=jnp.float32)
        )
        terms.append(
            -lax.dot_general(
                adjoint[-1], panels[:, columns], contract, precision=mode, preferred_element_type=jnp.float32
            )
        )
    diag_adjoint = lax.psum_scatter(jnp.stack(terms), "row", scatter_dimension=1, tiled=True)
    return jnp.concatenate(adjoint, axis=1), diag_adjoint


def solution(mesh):
    in_specs = (P("row", "col"), P("row", None), P("row", None), P())
    out_specs = (P("row", None), P(None, "row", None))
    on_ladder = mesh.shape["col"] == 2 and mesh.shape["row"] == 16
    return jax.shard_map(
        ladder_device if on_ladder else plain_device,
        mesh=mesh, in_specs=in_specs, out_specs=out_specs, check_vma=False,
    )
```

time: 122 us -> 109 us (0.89)
  Pallas kernels: 117 us -> 104 us
    pallas_call x1, Pallas kernels: 117 us -> 104 us  [ladder_device(): pl.pallas_call(kernel, out_shape=(jax.ShapeDtypeStruct(panels.shape, f32)...]
where the time goes in v1:
time: 109 us
  Pallas kernels  104 us (95%)
  local copies, waits for them, and re-layouts  3.85 us (4%)
    pallas_call x1, Pallas kernels, ladder_device(): pl.pallas_call(kernel, out_shape=(jax.ShapeDtypeStruct(panels.shape, f32)...  104 us
    unnamed x4, local copies, waits for them, and re-layouts  3.85 us

profile of v1, /device:TPU:0, one launch (start us, length us, event | category | flops | bytes accessed | tf_op | source)
XLA Modules:
  0.0 108.6 jit_solution(8953713430876266428)
XLA Ops:
  0.6 104.1 %shard_map.59 = (f32[512,1024]{1,0:T(8,128)}, f32[2,32,512]{2,1,0:T(8,128)}) custom-call(f32[512,4096]{1,0:T(8,128)} %refs_0_.1, f32[512,1024]{1,0:T(8,128)} %refs_1_.1, f32[512,1024]{1,0:T(8,128)} %refs_2_.1, f32[2,512,512]{2,1,0:T(8,128)} %refs_3_.1), custom_call_target="tpu_custom_call" | custom-call | tf_op jit(solution)/shard_map/pallas_call | solution.py:685
  104.7 0.0 copy-start
  104.7 3.2 %copy.8 = f32[512,1024]{1,0:T(8,128)} copy(f32[512,1024]{1,0:T(8,128)} %get-tuple-element.4) | data formatting | bytes 4194304
  107.9 0.0 copy-done
  107.9 0.7 copy.9
Async XLA Ops:
  104.7 3.2 %copy-start = (f32[2,32,512]{2,1,0:T(8,128)S(1)}, f32[2,32,512]{2,1,0:T(8,128)}, u32[]{:S(2)}) copy-start(f32[2,32,512]{2,1,0:T(8,128)} %get-tuple-element.5) | copy-start | bytes 393220

commit v2 on v1

v2 whole, which is shorter than its diff:
```python
import jax
import jax.numpy as jnp
from jax import lax
from jax.experimental import pallas as pl
from jax.experimental.pallas import tpu as pltpu
from jax.sharding import PartitionSpec as P

MESH = pl.DeviceIdType.MESH
SUBS = 4
UP, DOWN, ACROSS = 0, 1, 2
EARLY, COMB, LATE = 0, 1, 2
PAIRED = 96


def halves(value):
    high = value.astype(jnp.bfloat16)
    low = (value - high.astype(jnp.float32)).astype(jnp.bfloat16)
    return high, low


def product(left, right):
    (left_high, left_low), (right_high, right_low) = left, right

    def one(a, b):
        return jnp.dot(a, b, preferred_element_type=jnp.float32)

    return one(left_high, right_low) + one(left_low, right_high) + one(left_high, right_high)


def ladder_kernel(
    nz, gbar, panels, cot, inverses,
    adjoint, diag,
    g_v, p_v, gath_spine, gath_comb, terms, other, zin_pair, zin_one, xin_one, xin_last, final,
    acc_spine, acc_comb, acc_spine_other, acc_comb_other, p_high, p_low, inv_v, cot_t, adj_v,
    diag_v, diag_mate, diag_parts, diag_out,
    load_sems, own_sems, out_sems,
    gath_send, gath_recv, gath_mate,
    term_sems, xone_sems, pair_send, pair_recv, one_send, one_recv, last_sems,
    end_send, end_recv, acc_sems,
    mate_sems, part_send, part_recv, swap_sems,
):
    width = inverses.shape[-1]
    chips = 2 * nz
    half = width // 2
    lane = half
    row = lax.axis_index("row")
    col = lax.axis_index("col")
    chip = row // 2
    core = row % 2
    mate = 1 - core
    x = chip % 2
    z = chip // 2
    across = 2 * z + 1 - x

    def port_chip(port):
        if isinstance(port, int) and port == ACROSS:
            return across
        return chip + 2 - 4 * port

    def has_next(port):
        return jnp.where(port == UP, z < nz - 1, z > 0)

    def has_prev(port):
        return jnp.where(port == UP, z > 0, z < nz - 1)

    def behind(port, step):
        return z - step + 2 * step * port

    def ahead(port, step):
        return z + step - 2 * step * port

    def inside(place):
        return (place >= 0) & (place < nz)

    def load_g(tile):
        start = pl.multiple_of(tile * width, width)
        return pltpu.make_async_copy(gbar.at[:, pl.ds(start, width)], g_v.at[tile], load_sems.at[tile])

    def load_p(panel):
        columns = slice(panel * width, (panel + 1) * width)
        return pltpu.make_async_copy(panels.at[:, columns], p_v.at[:, columns], load_sems.at[chips + panel])

    def columns_of(side):
        quarter = width // 4
        return {EARLY: slice(0, quarter), LATE: slice(quarter, half), COMB: slice(half, width)}[side]

    def gath(tile, side):
        return gath_comb.at[tile] if side == COMB else gath_spine.at[side // 2, tile]

    def acc(side):
        return acc_comb if side == COMB else acc_spine.at[side // 2]

    def acc_other(side):
        return acc_comb_other if side == COMB else acc_spine_other.at[side // 2]

    def load_own(side):
        return pltpu.make_async_copy(panels.at[:, columns_of(side)], gath(chip, side), own_sems.at[side])

    load_cot = pltpu.make_async_copy(cot, adj_v, load_sems.at[chips + 2])
    load_inv = pltpu.make_async_copy(inverses, inv_v, load_sems.at[chips + 3])

    def order(count):
        place = jnp.where(z < nz // 2, nz - 1 - count // 2, count // 2)
        return 2 * place + jnp.where(count % 2 == 0, 1 - x, x)

    @pl.when(core == col)
    def _():
        for side in (EARLY, COMB, LATE):
            load_own(side).start()

    load_p(1).start()
    for count in range(chips):
        load_g(order(count)).start()
    load_p(0).start()
    load_cot.start()
    load_inv.start()

    barrier = pltpu.get_barrier_semaphore()
    friends = [
        (2 * across + core, col),
        (2 * chip + mate, col),
        (2 * chip + core, 1 - col),
        (2 * chip + mate, 1 - col),
    ]

    def greet(friend):
        pl.semaphore_signal(barrier, inc=1, device_id=friend, device_id_type=MESH)

    for friend in friends:
        greet(friend)
    for port in (UP, DOWN):
        pl.when(has_next(port))(lambda: greet((2 * port_chip(port) + core, col)))

    pl.semaphore_wait(barrier, len(friends) + jnp.where((z > 0) & (z < nz - 1), 2, 1))

    def gather_copy(tile, side, port):
        rows = pl.ds(pl.multiple_of(core * half, half), half)
        return pltpu.make_async_remote_copy(
            gath(tile, side).at[rows],
            gath(tile, side).at[rows],
            gath_send.at[port, tile, side],
            gath_recv.at[tile, side],
            device_id=(2 * port_chip(port) + core, col),
            device_id_type=MESH,
        )

    def gather_pair(tile, side):
        rows = pl.ds(pl.multiple_of(core * half, half), half)
        return pltpu.make_async_remote_copy(
            gath(tile, side).at[rows],
            gath(tile, side).at[rows],
            gath_mate.at[0, tile, side],
            gath_mate.at[1, tile, side],
            device_id=(2 * chip + mate, col),
            device_id_type=MESH,
        )

    def gather_own_pair(side):
        return pltpu.make_async_remote_copy(
            gath(chip, side),
            gath(chip, side),
            gath_mate.at[0, chip, side],
            gath_mate.at[1, chip, side],
            device_id=(2 * chip + mate, col),
            device_id_type=MESH,
        )

    def own_sends(act, routes, sides):
        @pl.when(core == col)
        def _():
            for side in sides:
                act(gather_own_pair(side))

        for side, port in routes:
            if side in sides and act is start:
                @pl.when(core != col)
                def _():
                    gather_own_pair(side).wait_recv()

                sides = tuple(other for other in sides if other != side)
            copy = gather_copy(chip, side, port)
            if port == ACROSS:
                act(copy)
            else:
                pl.when(has_next(port))(lambda: act(copy))

    first_routes = [(EARLY, ACROSS), (COMB, UP), (COMB, DOWN), (EARLY, UP), (EARLY, DOWN), (COMB, ACROSS)]

    def own_first(act):
        own_sends(act, first_routes, (EARLY, COMB))

    def own_across(act):
        own_sends(act, [(LATE, ACROSS)], (LATE,))

    def own_along(act):
        own_sends(act, [(LATE, UP), (LATE, DOWN)], ())

    def relay(tile, side, ports, act):
        for port in ports:
            if port == ACROSS:
                act(gather_copy(tile, side, port))
            else:
                @pl.when(has_next(port))
                def _():
                    act(gather_copy(tile, side, port))
        act(gather_pair(tile, side))

    def arrived(tile, side):
        gather_copy(tile, side, ACROSS).wait_recv()

    def start(copy):
        copy.start()

    def finish(copy):
        copy.wait_send()

    def relay_b(step, act):
        for port in (UP, DOWN):
            place = behind(port, step)

            @pl.when(inside(place))
            def _():
                tile = 2 * place + x
                if act is start:
                    arrived(tile, COMB)
                relay(tile, COMB, (port, ACROSS), act)

    def relay_a(step, act, own, part):
        for port in (UP, DOWN):
            place = behind(port, step)

            @pl.when(inside(place))
            def _():
                tile = 2 * place + (x if own else 1 - x)
                if act is start:
                    arrived(tile, part)
                relay(tile, part, (port,), act)

    def relay_a_across(act, part):
        if act is start:
            arrived(across, part)
        relay(across, part, (UP, DOWN), act)

    def relay_bx(step, act):
        for port in (UP, DOWN) if step else (UP,):
            place = behind(port, step)

            @pl.when(inside(place))
            def _():
                tile = 2 * place + 1 - x
                if act is start:
                    arrived(tile, COMB)
                relay(tile, COMB, (), act)

    def forward(tile, side):
        @pl.when(tile != chip)
        def _():
            gather_pair(tile, side).wait_recv()

        acc(side)[...] += product(halves(g_v[tile]), halves(gath(tile, side)[...]))

    def forward_step(step, kinds):
        def both(port, carry):
            place = behind(port, step)

            @pl.when(inside(place))
            def _():
                for side, own in kinds:
                    forward(2 * place + (x if own else 1 - x), side)

            return carry

        lax.fori_loop(0, 2 if step else 1, both, 0)

    def term_copy(tile):
        return pltpu.make_async_remote_copy(
            terms.at[tile, mate],
            other.at[tile],
            term_sems.at[0, tile],
            term_sems.at[1, tile],
            device_id=(2 * chip + mate, col),
            device_id_type=MESH,
        )

    def xone_copy(place, tile):
        return pltpu.make_async_remote_copy(
            terms.at[tile, core, pl.ds(PAIRED, lane - PAIRED)],
            xin_one.at[place],
            xone_sems.at[0, place],
            xone_sems.at[1, place],
            device_id=(2 * across + core, col),
            device_id_type=MESH,
        )

    def make_terms(count):
        tile = order(count)
        load_g(tile).wait()
        for part in (0, 1):
            rows = slice(part * half, (part + 1) * half)
            value = product((p_high[rows, :], p_low[rows, :]), halves(g_v[tile]))
            terms[tile, part] = value
        term_copy(tile).start()

    def pair_terms(count):
        tile = order(count)
        term_copy(tile).wait_recv()
        terms[tile, core] = terms[tile, core] + other[tile]

        @pl.when(count == 0)
        def _():
            xone_copy(tile // 2, tile).start()

    def send_across(count):
        tile = order(count)
        xone_copy(tile // 2, tile).start()

    def pieces(part, sub):
        size = (lane - PAIRED if part else PAIRED) // SUBS
        start = sub * size if isinstance(sub, int) else pl.multiple_of(sub * size, 8)
        return pl.ds(start, size), pl.ds(start + part * PAIRED, size)

    def pair_copy(port, step, slot, tile, sub):
        rows, _ = pieces(0, sub)
        return pltpu.make_async_remote_copy(
            terms.at[tile, core, rows],
            zin_pair.at[port, step - 1, slot, rows],
            pair_send.at[port, step - 1, slot, sub],
            pair_recv.at[port, step - 1, slot, sub],
            device_id=(2 * port_chip(port) + core, col),
            device_id_type=MESH,
        )

    def one_copy(port, step, tile, sub):
        rows, held = pieces(1, sub)
        return pltpu.make_async_remote_copy(
            terms.at[tile, core, held],
            zin_one.at[port, step - 1, rows],
            one_send.at[port, step - 1, sub],
            one_recv.at[port, step - 1, sub],
            device_id=(2 * port_chip(port) + core, col),
            device_id_type=MESH,
        )

    def sum_pair(step):
        for slot in (0, 1):
            for port in (UP, DOWN):
                place = ahead(port, step)

                @pl.when(inside(place))
                def _():
                    tile = 2 * place + (x if slot else 1 - x)

                    def each(sub, carry):
                        rows, _ = pieces(0, sub)
                        if step < nz - 1:
                            @pl.when(has_prev(port))
                            def _():
                                pair_copy(port, step + 1, slot, tile, sub).wait_recv()
                                terms[tile, core, rows] = (
                                    terms[tile, core, rows] + zin_pair[port, step, slot, rows]
                                )

                        pair_copy(port, step, slot, tile, sub).start()
                        return carry

                    lax.fori_loop(0, SUBS, each, 0)

    def sum_one(step):
        for port in (UP, DOWN):
            place = ahead(port, step)

            @pl.when(inside(place))
            def _():
                tile = 2 * place + x
                xone_copy(place, tile).wait_recv()

                def each(sub, carry):
                    rows, held = pieces(1, sub)
                    value = terms[tile, core, held] + xin_one[place, rows]
                    terms[tile, core, held] = value
                    if step < nz - 1:
                        @pl.when(has_prev(port))
                        def _():
                            one_copy(port, step + 1, tile, sub).wait_recv()
                            terms[tile, core, held] = value + zin_one[port, step, rows]

                    one_copy(port, step, tile, sub).start()
                    return carry

                lax.fori_loop(0, SUBS, each, 0)

    def last_copy(sub):
        rows, _ = pieces(0, sub)
        return pltpu.make_async_remote_copy(
            terms.at[across, core, rows],
            xin_last.at[rows],
            last_sems.at[0, sub],
            last_sems.at[1, sub],
            device_id=(2 * across + core, col),
            device_id_type=MESH,
        )

    def end_copy(part, plane, source_core, sub):
        _, held = pieces(part, sub)
        return pltpu.make_async_remote_copy(
            terms.at[chip, source_core, held],
            final.at[source_core, held],
            end_send.at[part, plane, sub],
            end_recv.at[part, source_core, sub],
            device_id=(2 * chip + col, col if plane == 0 else 1 - col),
            device_id_type=MESH,
        )

    def end_local(part, source_core, sub):
        _, held = pieces(part, sub)
        return pltpu.make_async_copy(
            terms.at[chip, source_core, held],
            final.at[source_core, held],
            end_recv.at[part, source_core, sub],
        )

    def give_end(part, sub):
        end_copy(part, 1, core, sub).start()

        @pl.when(core == col)
        def _():
            end_local(part, core, sub).start()

        @pl.when(core != col)
        def _():
            end_copy(part, 0, core, sub).start()

    def last_pair(sub, carry):
        rows, _ = pieces(0, sub)
        for slot in (0, 1):
            tile = chip if slot else across
            for port in (UP, DOWN):
                @pl.when(has_prev(port))
                def _():
                    pair_copy(port, 1, slot, tile, sub).wait_recv()
                    terms[tile, core, rows] = terms[tile, core, rows] + zin_pair[port, 0, slot, rows]

            if slot == 0:
                last_copy(sub).start()

        @pl.when(sub > 0)
        def _():
            last_across(sub - 1, carry)

        return carry

    def last_across(sub, carry):
        rows, _ = pieces(0, sub)
        last_copy(sub).wait_recv()
        terms[chip, core, rows] = terms[chip, core, rows] + xin_last[rows]
        give_end(0, sub)
        return carry

    def last_one(sub, carry):
        rows, held = pieces(1, sub)
        terms[chip, core, held] = terms[chip, core, held] + xin_one[z, rows]
        for port in (UP, DOWN):
            @pl.when(has_prev(port))
            def _():
                one_copy(port, 1, chip, sub).wait_recv()
                terms[chip, core, held] = terms[chip, core, held] + zin_one[port, 0, rows]

        give_end(1, sub)
        return carry

    def drain_early():
        own_first(finish)
        own_across(finish)
        own_along(finish)
        relay_a_across(finish, EARLY)
        relay_a_across(finish, LATE)
        relay_bx(0, finish)

        def drain_terms(count, carry):
            tile = order(count)
            term_copy(tile).wait_send()

            @pl.when(tile % 2 != x)
            def _():
                xone_copy(tile // 2, tile).wait_send()

            return carry

        lax.fori_loop(0, chips, drain_terms, 0)
        for step in range(1, nz):
            relay_b(step, finish)
            for part in (EARLY, LATE):
                relay_a(step, finish, True, part)
                relay_a(step, finish, False, part)
            relay_bx(step, finish)

    def drain_step(step):
        def both(port, carry):
            place = ahead(port, step)

            @pl.when(inside(place))
            def _():
                def each(sub, carry):
                    for slot in (0, 1):
                        pair_copy(port, step, slot, 2 * place + (x if slot else 1 - x), sub).wait_send()
                    one_copy(port, step, 2 * place + x, sub).wait_send()
                    return carry

                lax.fori_loop(0, SUBS, each, 0)

            return carry

        lax.fori_loop(0, 2, both, 0)

    def acc_copy(side):
        return pltpu.make_async_remote_copy(
            acc(side),
            acc_other(side),
            acc_sems.at[0, side],
            acc_sems.at[1, side],
            device_id=(2 * chip + core, 1 - col),
            device_id_type=MESH,
        )

    side_columns = pl.ds(pl.multiple_of(col * half, half), half)
    short = width // (2 * chips)

    def mate_copy(panel):
        return pltpu.make_async_remote_copy(
            diag_v.at[panel, :, mate],
            diag_mate.at[panel],
            mate_sems.at[0, panel],
            mate_sems.at[1, panel],
            device_id=(2 * chip + mate, col),
            device_id_type=MESH,
        )

    def part_copy(panel, source, target):
        return pltpu.make_async_remote_copy(
            diag_v.at[panel, target, core],
            diag_parts.at[panel, source],
            part_send.at[panel, target],
            part_recv.at[panel, source],
            device_id=(2 * target + core, col),
            device_id_type=MESH,
        )

    def swap_copy(panel):
        return pltpu.make_async_remote_copy(
            diag_out.at[panel, :, side_columns],
            diag_out.at[panel, :, side_columns],
            swap_sems.at[0, panel],
            swap_sems.at[1, panel],
            device_id=(2 * chip + core, 1 - col),
            device_id_type=MESH,
        )

    def adjoint_out(panel):
        columns = slice(panel * width, (panel + 1) * width)
        return pltpu.make_async_copy(adj_v.at[:, columns], adjoint.at[:, columns], out_sems.at[panel])

    def solve_first():
        for side in (EARLY, COMB, LATE):
            acc_copy(side).wait_recv()
            columns = columns_of(side)
            cot_t[0, :, columns] = adj_v[:, columns] - 2.0 * (acc(side)[...] + acc_other(side)[...])
        turned = product(halves(cot_t[0]), halves(inv_v[0]))
        adj_v[:, :width] = turned
        adjoint_out(0).start()
        cot_t[0] = turned.T

    def solve_second():
        for part in (0, 1):
            for source in (0, 1):
                for sub in range(SUBS):
                    end_local(part, source, sub).wait()
        coupled = final[...].reshape(width, width)
        cot_t[1] = product(halves(inv_v[1]), halves(cot_t[1] - 2.0 * coupled))

    def turn_cot():
        cot_t[1] = adj_v[:, width:].T

    def turn_inv():
        inv_v[1] = inv_v[1].T

    def diagonal(panel):
        place = pl.multiple_of(panel * width + col * half, half)
        own = p_v[:, pl.ds(place, half)]
        value = -product(halves(cot_t[panel]), halves(own))
        diag_v[panel] = value.reshape(chips, 2, short, half)
        mate_copy(panel).start()

    def give_second():
        adj_v[:, width:] = cot_t[1].T
        adjoint_out(1).start()

    def scatter(panel):
        mate_copy(panel).wait_recv()
        diag_v[panel, :, core] = diag_v[panel, :, core] + diag_mate[panel]
        for hop in range(1, chips):
            part_copy(panel, chip, (chip + hop) % chips).start()

    def collect(panel):
        total = diag_v[panel, chip, core]
        for hop in range(1, chips):
            source = (chip + hop) % chips
            part_copy(panel, source, chip).wait_recv()
            total = total + diag_parts[panel, source]
        diag_out[panel, :, side_columns] = total
        swap_copy(panel).start()

    @pl.when(core == col)
    def _():
        for side in (EARLY, COMB, LATE):
            load_own(side).wait()

    own_first(start)
    load_p(1).wait()
    for part in (0, 1):
        rows = slice(part * half, (part + 1) * half)
        high, low = halves(p_v[:, width + part * half:width + (part + 1) * half].T)
        p_high[rows, :] = high
        p_low[rows, :] = low
    acc_spine[...] = jnp.zeros_like(acc_spine)
    acc_comb[...] = jnp.zeros_like(acc_comb)
    chores = {
        3: lambda: (relay_a_across(start, EARLY),)[-1],
        7: lambda: (relay_a(1, start, True, EARLY), relay_b(1, start),)[-1],
    }

    def produce(count, carry):
        make_terms(count)
        pl.when(count > 0)(lambda: pair_terms(count - 1))
        for at, chore in chores.items():
            pl.when(count == at)(chore)
        return carry

    lax.fori_loop(0, chips, produce, 0)
    pair_terms(jnp.int32(chips - 1))

    own_across(start)
    relay_a(1, start, False, EARLY)
    sum_pair(3)
    relay_b(2, start)
    relay_bx(0, start)
    sum_pair(2)
    forward_step(1, [(EARLY, False)])
    relay_a(2, start, True, EARLY)
    send_across(2)
    forward_step(0, [(COMB, True)])
    relay_a(2, start, False, EARLY)
    forward_step(1, [(EARLY, True)])
    forward_step(0, [(COMB, False)])
    forward_step(2, [(EARLY, False), (COMB, True), (EARLY, True)])
    forward_step(0, [(EARLY, False)])
    relay_a_across(start, LATE)
    forward_step(0, [(EARLY, True)])
    relay_b(3, start)
    forward_step(3, [(COMB, True)])
    relay_a(3, start, True, EARLY)
    own_along(start)
    sum_one(3)
    forward_step(3, [(EARLY, True)])
    relay_bx(2, start)
    relay_bx(1, start)
    send_across(6)
    relay_a(3, start, False, EARLY)
    forward_step(3, [(EARLY, False)])
    relay_a(1, start, False, LATE)
    forward_step(1, [(COMB, True)])
    acc_copy(EARLY).start()
    relay_a(1, start, True, LATE)
    forward_step(0, [(LATE, False)])
    forward_step(2, [(COMB, False)])
    forward_step(1, [(COMB, False)])
    sum_one(2)
    relay_bx(3, start)
    forward_step(3, [(COMB, False)])
    acc_copy(COMB).start()
    relay_a(2, start, True, LATE)
    relay_a(2, start, False, LATE)
    forward_step(1, [(LATE, True)])
    send_across(4)
    sum_pair(1)
    forward_step(0, [(LATE, True)])
    forward_step(2, [(LATE, False)])
    relay_a(3, start, True, LATE)
    relay_a(3, start, False, LATE)
    forward_step(3, [(LATE, True)])
    forward_step(2, [(LATE, True)])
    forward_step(3, [(LATE, False)])
    forward_step(1, [(LATE, False)])
    acc_copy(LATE).start()
    sum_one(1)
    load_p(0).wait()
    load_cot.wait()
    load_inv.wait()
    turn_cot()
    turn_inv()
    drain_early()
    drain_step(3)
    drain_step(2)
    lax.fori_loop(0, SUBS, last_pair, 0)
    last_across(SUBS - 1, 0)
    xone_copy(z, chip).wait_recv()
    lax.fori_loop(0, SUBS, last_one, 0)
    solve_first()
    diagonal(0)
    scatter(0)
    drain_step(1)
    for sub in range(SUBS):
        last_copy(sub).wait_send()
    for side in (EARLY, COMB, LATE):
        acc_copy(side).wait_send()
    solve_second()
    diagonal(1)
    collect(0)
    scatter(1)
    give_second()
    collect(1)

    for sub in range(SUBS):
        for part in (0, 1):
            end_copy(part, 1, core, sub).wait_send()

            @pl.when(core != col)
            def _():
                end_copy(part, 0, core, sub).wait_send()

    for panel in (0, 1):
        mate_copy(panel).wait_send()
        for hop in range(1, chips):
            part_copy(panel, chip, (chip + hop) % chips).wait_send()
        swap_copy(panel).wait()
        adjoint_out(panel).wait()
    store = pltpu.make_async_copy(diag_out, diag, out_sems.at[2])
    store.start()
    store.wait()


def ladder_device(gbar, panels, panel_cot, inverses):
    width = inverses.shape[-1]
    chips = lax.axis_size("row") // 2
    nz = chips // 2
    half = width // 2
    short = width // (2 * chips)
    f32, bf16, dma = jnp.float32, jnp.bfloat16, pltpu.SemaphoreType.DMA
    anywhere = pl.BlockSpec(memory_space=pl.ANY)

    def kernel(*refs):
        ladder_kernel(nz, *refs)

    return pl.pallas_call(
        kernel,
        out_shape=(
            jax.ShapeDtypeStruct(panels.shape, f32),
            jax.ShapeDtypeStruct((2, short, width), f32),
        ),
        in_specs=[anywhere] * 4,
        out_specs=(anywhere, anywhere),
        scratch_shapes=[
            pltpu.VMEM((chips, width, width), f32),
            pltpu.VMEM(panels.shape, f32),
            pltpu.VMEM((2, chips, width, width // 4), f32),
            pltpu.VMEM((chips, width, half), f32),
            pltpu.VMEM((chips, 2, half, width), f32),
            pltpu.VMEM((chips, half, width), f32),
            pltpu.VMEM((2, nz - 1, 2, PAIRED, width), f32),
            pltpu.VMEM((2, nz - 1, half - PAIRED, width), f32),
            pltpu.VMEM((nz, half - PAIRED, width), f32),
            pltpu.VMEM((PAIRED, width), f32),
            pltpu.VMEM((2, half, width), f32),
            pltpu.VMEM((2, width, width // 4), f32),
            pltpu.VMEM((width, half), f32),
            pltpu.VMEM((2, width, width // 4), f32),
            pltpu.VMEM((width, half), f32),
            pltpu.VMEM((width, width), bf16),
            pltpu.VMEM((width, width), bf16),
            pltpu.VMEM(inverses.shape, f32),
            pltpu.VMEM(inverses.shape, f32),
            pltpu.VMEM(panels.shape, f32),
            pltpu.VMEM((2, chips, 2, short, half), f32),
            pltpu.VMEM((2, chips, short, half), f32),
            pltpu.VMEM((2, chips, short, half), f32),
            pltpu.VMEM((2, short, width), f32),
            dma((chips + 4,)),
            dma((3,)),
            dma((3,)),
            dma((3, chips, 3)),
            dma((chips, 3)),
            dma((2, chips, 3)),
            dma((2, chips)),
            dma((2, nz)),
            dma((2, nz - 1, 2, SUBS)),
            dma((2, nz - 1, 2, SUBS)),
            dma((2, nz - 1, SUBS)),
            dma((2, nz - 1, SUBS)),
            dma((2, SUBS)),
            dma((2, 2, SUBS)),
            dma((2, 2, SUBS)),
            dma((2, 3)),
            dma((2, 2)),
            dma((2, chips)),
            dma((2, chips)),
            dma((2, 2)),
        ],
        compiler_params=pltpu.CompilerParams(
            collective_id=0, has_side_effects=True, vmem_limit_bytes=62 * 1024 * 1024
        ),
    )(gbar, panels, panel_cot, inverses)


def plain_device(gbar, panels, panel_cot, inverses):
    width = inverses.shape[-1]
    mode = lax.Precision.HIGHEST
    row_id = lax.axis_index("row")
    col_count = lax.axis_size("col")
    contract = (((0,), (0,)), ((), ()))
    partial_value = lax.dot_general(
        gbar, panels, contract, precision=mode, preferred_element_type=jnp.float32
    )
    summed = lax.psum(partial_value, "row")
    own_tile = lax.dynamic_slice_in_dim(summed, row_id // col_count * width, width, 0)
    own_tile = jnp.where(lax.axis_index("col") == row_id % col_count, own_tile, 0)
    combined = panel_cot - 2.0 * lax.psum(own_tile, "col")
    adjoint, terms = [], []
    for panel in (0, 1):
        columns = slice(panel * width, (panel + 1) * width)
        adjoint.append(
            jnp.dot(combined[:, columns], inverses[panel], precision=mode, preferred_element_type=jnp.float32)
        )
        terms.append(
            -lax.dot_general(
                adjoint[-1], panels[:, columns], contract, precision=mode, preferred_element_type=jnp.float32
            )
        )
    diag_adjoint = lax.psum_scatter(jnp.stack(terms), "row", scatter_dimension=1, tiled=True)
    return jnp.concatenate(adjoint, axis=1), diag_adjoint


def solution(mesh):
    in_specs = (P("row", "col"), P("row", None), P("row", None), P())
    out_specs = (P("row", None), P(None, "row", None))
    on_ladder = mesh.shape["col"] == 2 and mesh.shape["row"] == 16
    return jax.shard_map(
        ladder_device if on_ladder else plain_device,
        mesh=mesh, in_specs=in_specs, out_specs=out_specs, check_vma=False,
    )
```

time: 109 us -> 105 us (0.963)
  Pallas kernels: 104 us -> 99.3 us
    pallas_call x1, Pallas kernels: 104 us -> 99.3 us  [ladder_device(): pl.pallas_call(kernel, out_shape=(jax.ShapeDtypeStruct(panels.shape, f32)...]
where the time goes in v2:
time: 105 us; the launch traced here: 104 us
  Pallas kernels  99.3 us (95%)
  local copies, waits for them, and re-layouts  3.85 us (4%)
    pallas_call x1, Pallas kernels, ladder_device(): pl.pallas_call(kernel, out_shape=(jax.ShapeDtypeStruct(panels.shape, f32)...  99.3 us
    unnamed x4, local copies, waits for them, and re-layouts  3.85 us

profile of v2, /device:TPU:0, one launch (start us, length us, event | category | flops | bytes accessed | tf_op | source)
XLA Modules:
  0.0 103.8 jit_solution(14059741276593669405)
XLA Ops:
  0.6 99.3 %shard_map.59 = (f32[512,1024]{1,0:T(8,128)}, f32[2,32,512]{2,1,0:T(8,128)}) custom-call(f32[512,4096]{1,0:T(8,128)} %refs_0_.1, f32[512,1024]{1,0:T(8,128)} %refs_1_.1, f32[512,1024]{1,0:T(8,128)} %refs_2_.1, f32[2,512,512]{2,1,0:T(8,128)} %refs_3_.1), custom_call_target="tpu_custom_call" | custom-call | tf_op jit(solution)/shard_map/pallas_call | solution.py:753
  100.0 0.0 copy-start
  100.0 3.2 %copy.8 = f32[512,1024]{1,0:T(8,128)} copy(f32[512,1024]{1,0:T(8,128)} %get-tuple-element.4) | data formatting | bytes 4194304
  103.2 0.0 copy-done
  103.2 0.7 copy.9
Async XLA Ops:
  100.0 3.2 %copy-start = (f32[2,32,512]{2,1,0:T(8,128)S(1)}, f32[2,32,512]{2,1,0:T(8,128)}, u32[]{:S(2)}) copy-start(f32[2,32,512]{2,1,0:T(8,128)} %get-tuple-element.5) | copy-start | bytes 393220

commit v3 on v2

--- a/solution.py
+++ b/solution.py
@@ -31,7 +31,7 @@
     nz, gbar, panels, cot, inverses,
     adjoint, diag,
     g_v, p_v, gath_spine, gath_comb, terms, other, zin_pair, zin_one, xin_one, xin_last, final,
-    acc_spine, acc_comb, acc_spine_other, acc_comb_other, p_high, p_low, inv_v, cot_t, adj_v,
+    acc_spine, acc_comb, acc_spine_other, acc_comb_other, p_high, p_low, inv_v, cot_t, adj_t, adj_v,
     diag_v, diag_mate, diag_parts, diag_out,
     load_sems, own_sems, out_sems,
     gath_send, gath_recv, gath_mate,
@@ -43,6 +43,7 @@
     chips = 2 * nz
     half = width // 2
     lane = half
+    split = width - 2 * PAIRED
     row = lax.axis_index("row")
     col = lax.axis_index("col")
     chip = row // 2
@@ -400,11 +401,16 @@
             device_id_type=MESH,
         )
 
+    def final_rows(part, source_core, sub):
+        size = lane - PAIRED if part else PAIRED
+        start = source_core * size + sub * (size // SUBS) + (0 if part else split)
+        return pl.ds(start if isinstance(start, int) else pl.multiple_of(start, 8), size // SUBS)
+
     def end_copy(part, plane, source_core, sub):
         _, held = pieces(part, sub)
         return pltpu.make_async_remote_copy(
             terms.at[chip, source_core, held],
-            final.at[source_core, held],
+            final.at[final_rows(part, source_core, sub)],
             end_send.at[part, plane, sub],
             end_recv.at[part, source_core, sub],
             device_id=(2 * chip + col, col if plane == 0 else 1 - col),
@@ -415,7 +421,7 @@
         _, held = pieces(part, sub)
         return pltpu.make_async_copy(
             terms.at[chip, source_core, held],
-            final.at[source_core, held],
+            final.at[final_rows(part, source_core, sub)],
             end_recv.at[part, source_core, sub],
         )
 
@@ -525,12 +531,16 @@
     side_columns = pl.ds(pl.multiple_of(col * half, half), half)
     short = width // (2 * chips)
 
-    def mate_copy(panel):
-        return pltpu.make_async_remote_copy(
-            diag_v.at[panel, :, mate],
-            diag_mate.at[panel],
-            mate_sems.at[0, panel],
-            mate_sems.at[1, panel],
+    bound = split // (2 * short)
+    groups = ((0, 0, chips), (1, bound, chips), (1, 0, bound))
+
+    def mate_copy(group):
+        panel, low, high = groups[group]
+        return pltpu.make_async_remote_copy(
+            diag_v.at[panel, low:high, mate],
+            diag_mate.at[panel, low:high],
+            mate_sems.at[0, group],
+            mate_sems.at[1, group],
             device_id=(2 * chip + mate, col),
             device_id_type=MESH,
         )
@@ -569,13 +579,21 @@
         adjoint_out(0).start()
         cot_t[0] = turned.T
 
-    def solve_second():
-        for part in (0, 1):
-            for source in (0, 1):
-                for sub in range(SUBS):
-                    end_local(part, source, sub).wait()
-        coupled = final[...].reshape(width, width)
-        cot_t[1] = product(halves(inv_v[1]), halves(cot_t[1] - 2.0 * coupled))
+    def wait_end(part):
+        for source in (0, 1):
+            for sub in range(SUBS):
+                end_local(part, source, sub).wait()
+
+    def solve_high():
+        wait_end(0)
+        cot_t[1, split:] = cot_t[1, split:] - 2.0 * final[split:]
+        first = split // 128 * 128
+        adj_t[split:] = product(halves(inv_v[1, split:, first:]), halves(cot_t[1, first:]))
+
+    def solve_low():
+        wait_end(1)
+        cot_t[1, :split] = cot_t[1, :split] - 2.0 * final[:split]
+        adj_t[:split] = product(halves(inv_v[1, :split]), halves(cot_t[1]))
 
     def turn_cot():
         cot_t[1] = adj_v[:, width:].T
@@ -583,22 +601,29 @@
     def turn_inv():
         inv_v[1] = inv_v[1].T
 
-    def diagonal(panel):
+    def diagonal(group):
+        panel, low, high = groups[group]
         place = pl.multiple_of(panel * width + col * half, half)
         own = p_v[:, pl.ds(place, half)]
-        value = -product(halves(cot_t[panel]), halves(own))
-        diag_v[panel] = value.reshape(chips, 2, short, half)
-        mate_copy(panel).start()
+        source = adj_t[2 * short * low:2 * short * high] if panel else cot_t[0]
+        value = -product(halves(source), halves(own))
+        diag_v[panel, low:high] = value.reshape(high - low, 2, short, half)
+        mate_copy(group).start()
 
     def give_second():
-        adj_v[:, width:] = cot_t[1].T
+        adj_v[:, width:] = adj_t[...].T
         adjoint_out(1).start()
 
-    def scatter(panel):
-        mate_copy(panel).wait_recv()
-        diag_v[panel, :, core] = diag_v[panel, :, core] + diag_mate[panel]
+    def scatter(group):
+        panel, low, high = groups[group]
+        mate_copy(group).wait_recv()
+        diag_v[panel, low:high, core] = diag_v[panel, low:high, core] + diag_mate[panel, low:high]
         for hop in range(1, chips):
-            part_copy(panel, chip, (chip + hop) % chips).start()
+            target = (chip + hop) % chips
+
+            @pl.when((target >= low) & (target < high))
+            def _():
+                part_copy(panel, chip, target).start()
 
     def collect(panel):
         total = diag_v[panel, chip, core]
@@ -616,11 +641,15 @@
 
     own_first(start)
     load_p(1).wait()
+    high, low = halves(p_v[:, width:].T)
     for part in (0, 1):
-        rows = slice(part * half, (part + 1) * half)
-        high, low = halves(p_v[:, width + part * half:width + (part + 1) * half].T)
-        p_high[rows, :] = high
-        p_low[rows, :] = low
+        for to, first, size in (
+            (part * half, split + part * PAIRED, PAIRED),
+            (part * half + PAIRED, part * (half - PAIRED), half - PAIRED),
+        ):
+            p_high[to:to + size, :] = high[first:first + size]
+            p_low[to:to + size, :] = low[first:first + size]
+
     acc_spine[...] = jnp.zeros_like(acc_spine)
     acc_comb[...] = jnp.zeros_like(acc_comb)
     chores = {
@@ -697,25 +726,28 @@
     load_inv.wait()
     turn_cot()
     turn_inv()
-    drain_early()
-    drain_step(3)
-    drain_step(2)
     lax.fori_loop(0, SUBS, last_pair, 0)
     last_across(SUBS - 1, 0)
+    solve_first()
+    diagonal(0)
     xone_copy(z, chip).wait_recv()
     lax.fori_loop(0, SUBS, last_one, 0)
-    solve_first()
-    diagonal(0)
     scatter(0)
+    solve_high()
+    diagonal(1)
+    scatter(1)
+    solve_low()
+    diagonal(2)
+    scatter(2)
     drain_step(1)
     for sub in range(SUBS):
         last_copy(sub).wait_send()
     for side in (EARLY, COMB, LATE):
         acc_copy(side).wait_send()
-    solve_second()
-    diagonal(1)
+    drain_early()
+    drain_step(3)
+    drain_step(2)
     collect(0)
-    scatter(1)
     give_second()
     collect(1)
 
@@ -727,8 +759,9 @@
             def _():
                 end_copy(part, 0, core, sub).wait_send()
 
+    for group in range(len(groups)):
+        mate_copy(group).wait_send()
     for panel in (0, 1):
-        mate_copy(panel).wait_send()
         for hop in range(1, chips):
             part_copy(panel, chip, (chip + hop) % chips).wait_send()
         swap_copy(panel).wait()
@@ -769,7 +802,7 @@
             pltpu.VMEM((2, nz - 1, half - PAIRED, width), f32),
             pltpu.VMEM((nz, half - PAIRED, width), f32),
             pltpu.VMEM((PAIRED, width), f32),
-            pltpu.VMEM((2, half, width), f32),
+            pltpu.VMEM((width, width), f32),
             pltpu.VMEM((2, width, width // 4), f32),
             pltpu.VMEM((width, half), f32),
             pltpu.VMEM((2, width, width // 4), f32),
@@ -778,6 +811,7 @@
             pltpu.VMEM((width, width), bf16),
             pltpu.VMEM(inverses.shape, f32),
             pltpu.VMEM(inverses.shape, f32),
+            pltpu.VMEM((width, width), f32),
             pltpu.VMEM(panels.shape, f32),
             pltpu.VMEM((2, chips, 2, short, half), f32),
             pltpu.VMEM((2, chips, short, half), f32),
@@ -799,7 +833,7 @@
             dma((2, 2, SUBS)),
             dma((2, 2, SUBS)),
             dma((2, 3)),
-            dma((2, 2)),
+            dma((2, 3)),
             dma((2, chips)),
             dma((2, chips)),
             dma((2, 2)),

time: 105 us -> 103 us (0.981); the launches traced: 104 us -> 103 us
  no operation moved by 1% of the time
where the time goes in v3:
time: 103 us
  Pallas kernels  98.8 us (96%)
  local copies, waits for them, and re-layouts  3.85 us (4%)
    pallas_call x1, Pallas kernels, ladder_device(): pl.pallas_call(kernel, out_shape=(jax.ShapeDtypeStruct(panels.shape, f32)...  98.8 us
    unnamed x4, local copies, waits for them, and re-layouts  3.85 us

profile of v3, /device:TPU:0, one launch (start us, length us, event | category | flops | bytes accessed | tf_op | source)
XLA Modules:
  0.0 103.3 jit_solution(3153671297034640253)
XLA Ops:
  0.6 98.8 %shard_map.59 = (f32[512,1024]{1,0:T(8,128)}, f32[2,32,512]{2,1,0:T(8,128)}) custom-call(f32[512,4096]{1,0:T(8,128)} %refs_0_.1, f32[512,1024]{1,0:T(8,128)} %refs_1_.1, f32[512,1024]{1,0:T(8,128)} %refs_2_.1, f32[2,512,512]{2,1,0:T(8,128)} %refs_3_.1), custom_call_target="tpu_custom_call" | custom-call | tf_op jit(solution)/shard_map/pallas_call | solution.py:786
  99.4 0.0 copy-start
  99.4 3.2 %copy.8 = f32[512,1024]{1,0:T(8,128)} copy(f32[512,1024]{1,0:T(8,128)} %get-tuple-element.4) | data formatting | bytes 4194304
  102.6 0.0 copy-done
  102.6 0.7 copy.9
Async XLA Ops:
  99.4 3.2 %copy-start = (f32[2,32,512]{2,1,0:T(8,128)S(1)}, f32[2,32,512]{2,1,0:T(8,128)}, u32[]{:S(2)}) copy-start(f32[2,32,512]{2,1,0:T(8,128)} %get-tuple-element.5) | copy-start | bytes 393220

commit v4 on v3

--- a/solution.py
+++ b/solution.py
@@ -6,7 +6,7 @@
 from jax.sharding import PartitionSpec as P
 
 MESH = pl.DeviceIdType.MESH
-SUBS = 4
+SUBS = 2
 UP, DOWN, ACROSS = 0, 1, 2
 EARLY, COMB, LATE = 0, 1, 2
 PAIRED = 96

time: 103 us -> 103 us (level); the launches traced: 103 us -> 102 us
  Pallas kernels: 98.8 us -> 97.4 us
    pallas_call x1, Pallas kernels: 98.8 us -> 97.4 us  [ladder_device(): pl.pallas_call(kernel, out_shape=(jax.ShapeDtypeStruct(panels.shape, f32)...]
where the time goes in v4:
time: 103 us; the launch traced here: 102 us
  Pallas kernels  97.4 us (95%)
  local copies, waits for them, and re-layouts  3.85 us (4%)
    pallas_call x1, Pallas kernels, ladder_device(): pl.pallas_call(kernel, out_shape=(jax.ShapeDtypeStruct(panels.shape, f32)...  97.4 us
    unnamed x4, local copies, waits for them, and re-layouts  3.85 us

profile of v4, /device:TPU:0, one launch (start us, length us, event | category | flops | bytes accessed | tf_op | source)
XLA Modules:
  0.0 101.9 jit_solution(14764726313818107027)
XLA Ops:
  0.6 97.4 %shard_map.59 = (f32[512,1024]{1,0:T(8,128)}, f32[2,32,512]{2,1,0:T(8,128)}) custom-call(f32[512,4096]{1,0:T(8,128)} %refs_0_.1, f32[512,1024]{1,0:T(8,128)} %refs_1_.1, f32[512,1024]{1,0:T(8,128)} %refs_2_.1, f32[2,512,512]{2,1,0:T(8,128)} %refs_3_.1), custom_call_target="tpu_custom_call" | custom-call | tf_op jit(solution)/shard_map/pallas_call | solution.py:786
  98.0 0.0 copy-start
  98.1 3.2 %copy.8 = f32[512,1024]{1,0:T(8,128)} copy(f32[512,1024]{1,0:T(8,128)} %get-tuple-element.4) | data formatting | bytes 4194304
  101.2 0.0 copy-done
  101.2 0.7 copy.9
Async XLA Ops:
  98.0 3.2 %copy-start = (f32[2,32,512]{2,1,0:T(8,128)S(1)}, f32[2,32,512]{2,1,0:T(8,128)}, u32[]{:S(2)}) copy-start(f32[2,32,512]{2,1,0:T(8,128)} %get-tuple-element.5) | copy-start | bytes 393220
